TPU v7x, 32 devices: a whole 2x2x4 slice. The times are simulated.
32 devices in a mesh: chan: 8 (over y, x, core), freq: 4 (over z).
Axes of the slice: x: 2, y: 2, z: 4, core: 2. Of those that a mesh axis runs over, the one named last changes fastest.
Arguments:
- raw: bfloat16 [1280, 8192], P('chan', 'freq')
- good_list: int32 [1024], P('chan'), may hold values from 0 to 159, as said below
- dest: int32 [1024], P('chan'), may hold values from 0 to 7, as said below
- order: int32 [4], replicated, may hold values from 0 to 7, as said below
- picks: int32 [4, 2], replicated, may hold values from 0 to 255, as said below
Outputs:
- corr: float32 [2048, 8, 512], P('chan', None, 'freq')
Inputs may be any that keep to these rules, and one draw needn't show every extreme that they name: `good_list`: the 128 entries of one device are distinct local rows of its 160 recorded rows. `dest`: the entries of one device name each block either exactly 32 times or not at all; each block is named by exactly half of the devices. `order`: the 4 entries are distinct blocks. Each pick names a slot of block order[t] that a listed channel fills; the picks of one step are distinct.
All inputs are finite; a program needn't handle non-finite values.
Results may differ from a plain program's by a relative error of at most 0.0061.
Values may be sent and summed in bfloat16 or wider, within the bound.
A program may use at most 64 MiB of HBM per device.

v0:
```python
import math

import jax
import jax.numpy as jnp
from jax import lax
from jax.sharding import PartitionSpec as P

W = 1024
LAGS = 512


power_floor = 0.1


def spread(value, axis, root):
    mine = lax.axis_index(axis) == root
    return lax.psum(jnp.where(mine, value, jnp.zeros_like(value)), axis)


def transform_table(bands):
    sample = jnp.arange(W, dtype=jnp.int32)[:, None]
    column = jnp.arange(W, dtype=jnp.int32)[None, :]
    width_band = W // bands
    half_band = width_band // 2
    band_index = column // width_band
    within = column % width_band
    half_index = within // half_band
    bin_index = band_index * half_band + within % half_band
    residue = jnp.mod(sample * bin_index, W).astype(jnp.float32)
    phase_rad = residue * (2.0 * math.pi / W)
    taper = 0.5 - 0.5 * jnp.cos(sample.astype(jnp.float32) * (2.0 * math.pi / W))
    entries = (
        jnp.where(half_index == 0, jnp.cos(phase_rad), -jnp.sin(phase_rad))
        * taper
        * (1.0 / math.sqrt(W))
    )
    return entries.astype(jnp.bfloat16)


def lag_rows(row_index, lag_index, half_band, scale):
    band_index = row_index // (2 * half_band)
    within = row_index % (2 * half_band)
    half_index = within // half_band
    bin_index = band_index * half_band + within % half_band
    lag_shift = lag_index - LAGS // 2
    residue = jnp.mod(bin_index[:, None] * lag_shift[None, :], W).astype(jnp.float32)
    phase_rad = residue * (2.0 * math.pi / W)
    entries = jnp.where(half_index[:, None] == 0, jnp.cos(phase_rad), -jnp.sin(phase_rad)) * scale
    return entries.astype(jnp.bfloat16)


def whiten(spectra):
    values = spectra.astype(jnp.float32)
    half_band = values.shape[-1] // 2
    real_part = values[..., :half_band]
    imag_part = values[..., half_band:]
    band_power = jnp.mean(real_part * real_part + imag_part * imag_part, axis=1, keepdims=True)
    factor = 1.0 / jnp.sqrt(jnp.maximum(band_power, power_floor))
    return (values * jnp.concatenate([factor, factor], axis=-1)).astype(jnp.bfloat16)


def cross(whitened, panels):
    half_band = whitened.shape[-1] // 2
    left_re, left_im = (whitened[..., :half_band], whitened[..., half_band:])
    right_re, right_im = (panels[..., :half_band], panels[..., half_band:])
    real_part = jnp.einsum("isf,jsf->ijf", left_re, right_re, preferred_element_type=jnp.float32)
    real_part = real_part + jnp.einsum(
        "isf,jsf->ijf", left_im, right_im, preferred_element_type=jnp.float32
    )
    imag_part = jnp.einsum("isf,jsf->ijf", left_im, right_re, preferred_element_type=jnp.float32)
    imag_part = imag_part - jnp.einsum(
        "isf,jsf->ijf", left_re, right_im, preferred_element_type=jnp.float32
    )
    return jnp.concatenate([real_part, imag_part], axis=-1).astype(jnp.bfloat16)


def body(raw, good_list, dest, order, picks):
    n_chan = lax.axis_size("chan")
    n_freq = lax.axis_size("freq")
    good_count = good_list.shape[0]
    raw_rows = raw.shape[0]
    capacity = 2 * good_count // n_chan
    slot_count = n_chan * capacity
    sub_count = raw.shape[1] // W
    positions = jnp.arange(good_count, dtype=jnp.int32)
    matching = dest[:, None] == dest[None, :]
    earlier_count = jnp.sum(
        jnp.logical_and(matching, positions[None, :] < positions[:, None]), axis=1
    )
    slot_index = dest * capacity + earlier_count
    slot_onehot = (slot_index[:, None] == jnp.arange(slot_count, dtype=jnp.int32)[None, :]).astype(
        jnp.bfloat16
    )
    row_onehot = (good_list[:, None] == jnp.arange(raw_rows, dtype=jnp.int32)[None, :]).astype(
        jnp.bfloat16
    )
    packer = lax.dot_general(
        slot_onehot, row_onehot, (((0,), (0,)), ((), ())), preferred_element_type=jnp.float32
    )
    outgoing = jnp.dot(packer.astype(jnp.bfloat16), raw, preferred_element_type=jnp.float32).astype(
        jnp.bfloat16
    )
    outgoing = outgoing.reshape(n_chan, capacity, sub_count, W)
    trans = transform_table(n_freq)
    spectra = jnp.einsum(
        "rcmw,wk->rcmk",
        lax.all_to_all(outgoing, "chan", split_axis=0, concat_axis=0, tiled=True),
        trans,
        preferred_element_type=jnp.float32,
    ).astype(jnp.bfloat16)
    spectra = spectra.reshape(slot_count, sub_count, n_freq, W // n_freq)
    whitened = whiten(lax.all_to_all(spectra, "freq", split_axis=2, concat_axis=1, tiled=True))
    total_sub = whitened.shape[1]
    width_band = whitened.shape[3]
    whitened = whitened.reshape(slot_count, total_sub, width_band)
    steps = order.shape[0]
    gathered = []
    for step in range(steps):
        chosen = jnp.take(whitened, picks[step], axis=0)
        gathered.append(spread(chosen, "chan", order[step]))
    panels = jnp.concatenate(gathered, axis=0)
    spectra_cross = cross(whitened, panels)
    scale = 1.0 / math.sqrt(total_sub * (W // 2))
    half_band = width_band // 2
    row_index = lax.axis_index("freq") * width_band + jnp.arange(width_band, dtype=jnp.int32)
    lag_table = lag_rows(row_index, jnp.arange(LAGS, dtype=jnp.int32), half_band, scale)
    partial_corr = jnp.einsum(
        "ijf,fl->ijl", spectra_cross, lag_table, preferred_element_type=jnp.float32
    )
    corr = lax.psum_scatter(partial_corr, "freq", scatter_dimension=2, tiled=True)
    return corr


def solution(mesh):
    placed = (P("chan", "freq"), P("chan"), P("chan"), P(), P())
    return jax.shard_map(
        body, mesh=mesh, in_specs=placed, out_specs=P("chan", None, "freq"), check_vma=False
    )
```

profile of v0, /device:TPU:0, one launch (start us, length us, event | category | flops | bytes accessed | tf_op | source)
XLA Modules:
  0.0 206.9 jit_solution(5138852653627311148)
XLA Ops:
  6.5 0.0 copy-start
  6.5 0.0 copy-start.2
  6.5 0.9 convert_reduce_fusion
  7.5 0.7 multiply_add_fusion
  8.1 0.0 copy-done
  8.1 1.4 convolution_convert_fusion
  9.5 0.8 reshape.254
  10.3 1.3 copy.57
  11.6 5.2 %all-to-all-start = ((bf16[8,32,2,1024]{3,1,2,0:T(8,128)(2,1)}), bf16[8,32,2,1024]{3,1,2,0:T(8,128)(2,1)S(1)}, u32[]{:S(2)}, u32[]{:S(2)}) async-start(bf16[8,32,2,1024]{3,1,2,0:T(8,128)(2,1)} %copy.57), calls=%async_computation | async-start | bytes 2097152 | tf_op jit(solution)/shard_map/all_to_all | solution.py:107
  16.8 0.0 copy-done.2
  16.9 0.7 fusion.77
  17.5 14.6 %all-to-all-done = bf16[8,32,2,1024]{3,1,2,0:T(8,128)(2,1)S(1)} async-done(((bf16[8,32,2,1024]{3,1,2,0:T(8,128)(2,1)}), bf16[8,32,2,1024]{3,1,2,0:T(8,128)(2,1)S(1)}, u32[]{:S(2)}, u32[]{:S(2)}) %all-to-all-start) | async-done | bytes 1048608 | tf_op jit(solution)/shard_map/all_to_all | solution.py:107
  32.2 17.7 %fusion.17 = bf16[8,32,2,1024]{3,1,2,0:T(8,128)(2,1)S(1)} fusion(bf16[8,32,2,1024]{3,1,2,0:T(8,128)(2,1)S(1)} %all-to-all-done, f32[1024]{0:T(1024)S(1)} %multiply_subtract_fusion, s32[1024]{0:T(1024)S(1)} %fusion.55, pred[1024]{0:T(1024)(128)(4,1)S(1)} %fusion.52), kind=kOutput, calls=%fused_computation.26 | convolution fusion | flops 1094189056 | bytes 2106368 | tf_op jit(solution)/shard_map/rcmw,wk->rcmk/dot_general | solution.py:105
  49.8 0.0 copy-start.1
  49.9 0.1 copy.58
  49.9 0.8 reshape.255
  50.8 1.1 copy.59
  51.9 4.9 %all-to-all-start.1 = ((bf16[256,2,4,256]{3,0,1,2:T(8,128)(2,1)}), bf16[256,2,4,256]{3,0,1,2:T(8,128)(2,1)}, u32[]{:S(2)}, u32[]{:S(2)}) async-start(bf16[256,2,4,256]{3,0,1,2:T(8,128)(2,1)} %copy.59), calls=%async_computation.1 | async-start | bytes 2097152 | tf_op jit(solution)/shard_map/all_to_all | solution.py:112
  56.7 0.0 reduce-scatter.2.cloned.1.call-start
  59.3 0.0 copy-done.1
  59.3 0.2 slice_reduce_fusion
  59.6 20.1 %all-to-all-done.1 = bf16[256,2,4,256]{3,0,1,2:T(8,128)(2,1)} async-done(((bf16[256,2,4,256]{3,0,1,2:T(8,128)(2,1)}), bf16[256,2,4,256]{3,0,1,2:T(8,128)(2,1)}, u32[]{:S(2)}, u32[]{:S(2)}) %all-to-all-start.1) | async-done | bytes 1048608 | tf_op jit(solution)/shard_map/all_to_all | solution.py:112
  79.8 1.4 bitcast_convert_fusion
  81.2 0.1 fusion.25
  81.4 0.1 copy.60
  81.5 2.0 copy.61
  83.6 1.8 multiply_convert_fusion.1
  85.4 1.3 copy.62
  86.6 0.5 gather_fusion.3
  87.2 0.5 gather_fusion.2
  87.8 0.5 gather_fusion.1
  88.3 0.5 gather_fusion
  88.9 0.1 select_select_fusion
  88.9 0.1 select_select_fusion.1
  89.0 0.1 select_select_fusion.3
  89.1 0.1 select_select_fusion.2
  89.2 24.2 %all-reduce = (bf16[2,8,256]{2,1,0:T(8,128)(2,1)S(1)}, bf16[2,8,256]{2,1,0:T(8,128)(2,1)S(1)}, bf16[2,8,256]{2,1,0:T(8,128)(2,1)S(1)}, bf16[2,8,256]{2,1,0:T(8,128)(2,1)S(1)}) all-reduce(bf16[2,8,256]{2,1,0:T(8,128)(2,1)S(1)} %select_select_fusion.3, ...), channel_id=1, replica_groups=mesh['chan'=8,'freq'=4] {'chan'}, use_global_device_ids=true, to_apply=%region_2.4 | all-reduce | flops 16384 | bytes 65536 | tf_op jit(solution)/shard_map/psum | solution.py:17
  113.4 0.2 copy.71
  113.6 1.3 fusion.31
  114.9 0.3 fusion.35
  115.2 0.2 copy.72
  115.4 1.5 fusion.22
  116.9 0.3 fusion.23
  117.2 0.1 pad_maximum_fusion
  117.3 4.8 %fusion.26 = f32[256,8,512]{2,0,1:T(8,128)} fusion(bf16[256,8,256]{0,1,2:T(8,128)(2,1)S(1)} %pad_maximum_fusion, s32[512]{0:T(512)S(1)} %iota_add_fusion, s32[256]{0:T(256)S(1)} %fusion.63, pred[256]{0:T(512)(128)(4,1)S(1)} %fusion.65), kind=kOutput, calls=%fused_computation.40 | convolution fusion | flops 539230208 | bytes 5246208 | tf_op jit(solution)/shard_map/ijf,fl->ijl/dot_general | solution.py:127
  122.1 0.0 reduce-scatter.2.cloned.1.call-update
  122.1 75.1 %reduce-scatter.2.cloned.1.call-done = f32[256,8,128]{2,0,1:T(8,128)} async-done(((f32[256,8,512]{2,0,1:T(8,128)}), f32[256,8,128]{2,0,1:T(8,128)}) %reduce-scatter.2.cloned.1.call-update) | async-done | bytes 1048592 | tf_op jit(solution)/shard_map/reduce_scatter | solution.py:130
  197.2 2.8 %copy.69 = f32[256,8,128]{2,1,0:T(8,128)} copy(f32[256,8,128]{2,0,1:T(8,128)} %reduce-scatter.2.cloned.1.call-done) | data formatting | bytes 2097152 | tf_op jit(solution)/shard_map/reduce_scatter | solution.py:130
  (21 shorter events, 0.2 us)
Async XLA Ops:
  6.5 1.6 copy-start
  6.5 10.3 %copy-start.2 = (s32[4]{0:T(128)S(1)}, s32[4]{0:T(128)}, u32[]{:S(2)}) copy-start(s32[4]{0:T(128)} %param.10) | copy-start | bytes 52
  11.6 20.6 %all-to-all-start = ((bf16[8,32,2,1024]{3,1,2,0:T(8,128)(2,1)}), bf16[8,32,2,1024]{3,1,2,0:T(8,128)(2,1)S(1)}, u32[]{:S(2)}, u32[]{:S(2)}) async-start(bf16[8,32,2,1024]{3,1,2,0:T(8,128)(2,1)} %copy.57), calls=%async_computation | async-start | bytes 2097152 | tf_op jit(solution)/shard_map/all_to_all | solution.py:107
  49.8 9.5 %copy-start.1 = (s32[4,2]{0,1:T(2,128)S(1)}, s32[4,2]{0,1:T(2,128)}, u32[]{:S(2)}) copy-start(s32[4,2]{0,1:T(2,128)} %param.11) | copy-start | bytes 100
  51.9 27.9 %all-to-all-start.1 = ((bf16[256,2,4,256]{3,0,1,2:T(8,128)(2,1)}), bf16[256,2,4,256]{3,0,1,2:T(8,128)(2,1)}, u32[]{:S(2)}, u32[]{:S(2)}) async-start(bf16[256,2,4,256]{3,0,1,2:T(8,128)(2,1)} %copy.59), calls=%async_computation.1 | async-start | bytes 2097152 | tf_op jit(solution)/shard_map/all_to_all | solution.py:112
  56.7 140.5 %reduce-scatter.2.cloned.1.call-start = ((), (), s32[]{:S(2)}) async-start(), calls=%async_computation.3 | async-start | bytes 5242880 | tf_op jit(solution)/shard_map/reduce_scatter | solution.py:130
Sparse Core Ops, SparseCore 0:
  122.2 74.9 reduce-scatter.1
where the time goes:
time: 207 us
  waiting for transfers between devices  110 us (53%)
  matrix products  27.2 us (13%)
  blocking collectives  24.2 us (12%)
  between operations  16.2 us (8%)
  local copies, waits for them, and re-layouts  13.8 us (7%)
  starting transfers between devices  10 us (5%)
  other arithmetic  5.51 us (3%)
    reduce_scatter x1, waiting for transfers between devices, body(): lax.psum_scatter(partial_corr, 'freq', scatter_dimension=2, tiled=True)  75.1 us
    psum x1, blocking collectives, spread(): return lax.psum(jnp.where(mine, value, jnp.zeros_like(value)), axis)  24.2 us
    all_to_all x1, waiting for transfers between devices, body(): lax.all_to_all(spectra, 'freq', split_axis=2, concat_axis=1, tiled=True)  20.1 us
    dot_general x1, matrix products, body(): jnp.einsum('rcmw,wk->rcmk', lax.all_to_all(outgoing, 'chan', split_axis=0...  17.7 us
    all_to_all x1, waiting for transfers between devices, body(): lax.all_to_all(outgoing, 'chan', split_axis=0, concat_axis=0, tiled=True)  14.6 us
    all_to_all x1, starting transfers between devices, body(): lax.all_to_all(outgoing, 'chan', split_axis=0, concat_axis=0, tiled=True)  5.17 us
    all_to_all x1, starting transfers between devices, body(): lax.all_to_all(spectra, 'freq', split_axis=2, concat_axis=1, tiled=True)  4.87 us
    dot_general x1, matrix products, body(): jnp.einsum('ijf,fl->ijl', spectra_cross, lag_table, preferred_element_typ...  4.83 us
  transfers between devices with their start and end apart: 3, of which 3 were waited for; matrix products, arithmetic and copies ran while one was open for 1% of the time, Pallas kernels for 0%

commit v1 on v0

v1 whole, which is shorter than its diff:
```python
import math

import jax
import jax.numpy as jnp
import ml_dtypes
import numpy as np
from jax import lax
from jax.sharding import PartitionSpec as P

W = 1024
LAGS = 512


power_floor = 0.1


def transform_table(bands):
    sample = np.arange(W, dtype=np.int64)[:, None]
    column = np.arange(W, dtype=np.int64)[None, :]
    width_band = W // bands
    half_band = width_band // 2
    within = column % width_band
    bin_index = (column // width_band) * half_band + within % half_band
    phase_rad = ((sample * bin_index) % W) * (2.0 * math.pi / W)
    taper = 0.5 - 0.5 * np.cos(sample * (2.0 * math.pi / W))
    entries = np.where(within < half_band, np.cos(phase_rad), -np.sin(phase_rad))
    return (entries * taper / math.sqrt(W)).astype(np.float32).astype(ml_dtypes.bfloat16)


def lag_rows(bands, scale):
    row_index = np.arange(W, dtype=np.int64)
    width_band = W // bands
    half_band = width_band // 2
    within = row_index % width_band
    bin_index = (row_index // width_band) * half_band + within % half_band
    lag_shift = np.arange(LAGS, dtype=np.int64) - LAGS // 2
    phase_rad = ((bin_index[:, None] * lag_shift[None, :]) % W) * (2.0 * math.pi / W)
    entries = np.where(within[:, None] < half_band, np.cos(phase_rad), -np.sin(phase_rad))
    return (entries * scale).astype(np.float32).astype(ml_dtypes.bfloat16)


def whiten(spectra):
    values = spectra.astype(jnp.float32)
    band_power = jnp.mean(jnp.sum(values * values, axis=-2, keepdims=True), axis=-3, keepdims=True)
    factor = 1.0 / jnp.sqrt(jnp.maximum(band_power, power_floor))
    return (values * factor).astype(jnp.bfloat16)


def body(raw, good_list, dest, order, picks):
    n_chan = lax.axis_size("chan")
    n_freq = lax.axis_size("freq")
    good_count = good_list.shape[0]
    raw_rows = raw.shape[0]
    capacity = 2 * good_count // n_chan
    slot_count = n_chan * capacity
    sub_count = raw.shape[1] // W
    total_sub = sub_count * n_freq
    steps, per_step = picks.shape
    sources = steps * per_step
    share = good_count // n_freq
    positions = jnp.arange(good_count, dtype=jnp.int32)
    matching = dest[:, None] == dest[None, :]
    earlier_count = jnp.sum(
        jnp.logical_and(matching, positions[None, :] < positions[:, None]), axis=1
    )
    slot_index = dest * capacity + earlier_count
    row_onehot = (good_list[:, None] == jnp.arange(raw_rows, dtype=jnp.int32)[None, :]).astype(
        jnp.bfloat16
    )
    slot_onehot = (jnp.arange(slot_count, dtype=jnp.int32)[:, None] == slot_index[None, :]).astype(
        jnp.bfloat16
    )
    block = jnp.repeat(order, per_step)
    pick = picks.reshape(sources)
    mine = pick // capacity == lax.axis_index("chan")
    source_slot = jnp.where(mine, block * capacity + pick % capacity, -1)
    source_onehot = (source_slot[:, None] == slot_index[None, :]).astype(jnp.bfloat16)

    good = jnp.dot(row_onehot, raw, preferred_element_type=jnp.float32).astype(jnp.bfloat16)
    panel_raw = jnp.dot(source_onehot, good, preferred_element_type=jnp.float32).astype(jnp.bfloat16)
    panel_raw = lax.psum(panel_raw, "chan")
    panel_raw = lax.all_gather(panel_raw.reshape(sources, sub_count, W), "freq", axis=1, tiled=True)

    rows = lax.all_to_all(
        good.reshape(n_freq, share, sub_count, W), "freq", split_axis=0, concat_axis=2, tiled=True
    )
    rows = rows.reshape(share, total_sub, W)
    trans = jnp.asarray(transform_table(n_freq))
    half_band = W // n_freq // 2

    def white(values):
        spectra = jnp.einsum("cmw,wk->cmk", values, trans, preferred_element_type=jnp.float32)
        spectra = spectra.astype(jnp.bfloat16).reshape(-1, total_sub, n_freq, 2, half_band)
        spectra = spectra.transpose(0, 1, 3, 2, 4).reshape(-1, total_sub, 2, W // 2)
        return whiten(spectra).astype(jnp.float32)

    panels = white(panel_raw)
    whitened = white(rows)
    left_re, left_im = whitened[:, None, :, 0], whitened[:, None, :, 1]
    right_re, right_im = panels[None, :, :, 0], panels[None, :, :, 1]
    real_part = jnp.sum(left_re * right_re + left_im * right_im, axis=2)
    imag_part = jnp.sum(left_im * right_re - left_re * right_im, axis=2)
    spectra_cross = jnp.concatenate([real_part, imag_part], axis=-1).astype(jnp.bfloat16)
    scale = 1.0 / math.sqrt(total_sub * (W // 2))
    table = lag_rows(n_freq, scale).reshape(n_freq, 2, half_band, LAGS)
    table = jnp.asarray(table.transpose(1, 0, 2, 3).reshape(W, LAGS))
    corr = jnp.einsum("ijf,fl->ijl", spectra_cross, table, preferred_element_type=jnp.float32)
    corr = lax.all_to_all(
        corr.astype(jnp.bfloat16), "freq", split_axis=2, concat_axis=0, tiled=True
    )
    lags = LAGS // n_freq
    placed = jnp.dot(
        slot_onehot, corr.reshape(good_count, sources * lags), preferred_element_type=jnp.float32
    ).astype(jnp.bfloat16)
    placed = placed.reshape(n_chan, capacity, sources, lags)
    received = lax.all_to_all(placed, "chan", split_axis=0, concat_axis=0, tiled=True)
    return received.reshape(slot_count, sources, lags).astype(jnp.float32)


def solution(mesh):
    placed = (P("chan", "freq"), P("chan"), P("chan"), P(), P())
    return jax.shard_map(
        body, mesh=mesh, in_specs=placed, out_specs=P("chan", None, "freq"), check_vma=False
    )
```

time: 207 us -> 89.9 us (0.43)
  waiting for transfers between devices: 110 us -> 0.01 us
  blocking collectives: 24.2 us -> 62 us
  matrix products: 27.2 us -> 5.27 us
  between operations: 16.2 us -> 0.21 us
  starting transfers between devices: 10 us -> 6.32 us
  local copies, waits for them, and re-layouts: 13.8 us -> 10.7 us
    reduce_scatter x1 -> x0, waiting for transfers between devices: 75.1 us -> none  [body(): lax.psum_scatter(partial_corr, 'freq', scatter_dimension=2, tiled=True)]
    all_to_all x2 -> x1, waiting for transfers between devices: 34.8 us -> 0.01 us  [body(): lax.all_to_all(good.reshape(n_freq, share, sub_count, W), 'freq', split_a...]
    all_to_all x0 -> x2, blocking collectives: none -> 24 us  [the longest x1 12.2 us: body(): lax.all_to_all(placed, 'chan', split_axis=0, concat_axis=0, tiled=True)]
    dot_general x7 -> x6, matrix products: 27.2 us -> 5.27 us  [the longest x2 3.32 us: white(): jnp.einsum('cmw,wk->cmk', values, trans, preferred_element_type=jnp.float32)]
    all_gather x0 -> x1, blocking collectives: none -> 13.8 us  [body(): lax.all_gather(panel_raw.reshape(sources, sub_count, W), 'freq', axis=1,...]
    all_to_all x2 -> x1, starting transfers between devices: 10 us -> 6.32 us  [body(): lax.all_to_all(good.reshape(n_freq, share, sub_count, W), 'freq', split_a...]
    reduce_sum x1 -> x3, other arithmetic: 0.14 us -> 3.44 us  [the longest x1 3.26 us: body(): real_part = jnp.sum(left_re * right_re + left_im * right_im, axis=2)]
    reduce_scatter x1 -> x0, local copies, waits for them, and re-layouts: 2.8 us -> none  [body(): lax.psum_scatter(partial_corr, 'freq', scatter_dimension=2, tiled=True)]
  transfers between devices with their start and end apart: 3 -> 1, of which waited for: 3 -> 0; matrix products, arithmetic and copies ran while one was open for 1% -> 2% of each run, Pallas kernels for 0% -> 0%
where the time goes in v1:
time: 89.9 us; the launch traced here: 89.4 us
  blocking collectives  62 us (69%)
  local copies, waits for them, and re-layouts  10.7 us (12%)
  starting transfers between devices  6.32 us (7%)
  matrix products  5.27 us (6%)
  other arithmetic  4.92 us (5%)
    psum x1, blocking collectives, body(): panel_raw = lax.psum(panel_raw, 'chan')  24.2 us
    all_gather x1, blocking collectives, body(): lax.all_gather(panel_raw.reshape(sources, sub_count, W), 'freq', axis=1,...  13.8 us
    all_to_all x1, blocking collectives, body(): lax.all_to_all(placed, 'chan', split_axis=0, concat_axis=0, tiled=True)  12.2 us
    all_to_all x1, blocking collectives, body(): lax.all_to_all(corr.astype(jnp.bfloat16), 'freq', split_axis=2, concat_ax...  11.8 us
    all_to_all x1, starting transfers between devices, body(): lax.all_to_all(good.reshape(n_freq, share, sub_count, W), 'freq', split_a...  6.32 us
    dot_general x2, matrix products, white(): jnp.einsum('cmw,wk->cmk', values, trans, preferred_element_type=jnp.float32)  3.32 us
    reduce_sum x1, other arithmetic, body(): real_part = jnp.sum(left_re * right_re + left_im * right_im, axis=2)  3.26 us
    unnamed x16, local copies, waits for them, and re-layouts  2.77 us
  transfers between devices with their start and end apart: 1, of which 0 were waited for; matrix products, arithmetic and copies ran while one was open for 2% of the time, Pallas kernels for 0%

profile of v1, /device:TPU:0, one launch (start us, length us, event | category | flops | bytes accessed | tf_op | source)
XLA Modules:
  0.0 89.4 jit_solution(17320880894635454601)
XLA Ops:
  0.0 0.0 copy-start
  0.0 0.0 copy-start.1
  0.0 0.0 copy-start.3
  0.0 0.0 copy-start.4
  0.0 1.1 %copy-done = bf16[160,2048]{1,0:T(8,128)(2,1)S(1)} copy-done((bf16[160,2048]{1,0:T(8,128)(2,1)S(1)}, bf16[160,2048]{1,0:T(8,128)(2,1)}, u32[]{:S(2)}) %copy-start) | copy-done | bytes 655384
  1.1 0.0 copy-start.2
  1.1 1.0 %convolution_convert_fusion = bf16[128,2048]{1,0:T(8,128)(2,1)S(1)} fusion(bf16[160,2048]{1,0:T(8,128)(2,1)S(1)} %copy-done, s32[128]{0:T(128)} %param.8), kind=kOutput, calls=%fused_computation.2 | convolution fusion | flops 84168704 | bytes 1180160 | tf_op jit(solution)/shard_map/dot_general | solution.py:79
  2.1 1.2 %reshape.152 = bf16[4,32,2,1024]{3,2,1,0:T(2,128)(2,1)} reshape(bf16[128,2048]{1,0:T(8,128)(2,1)S(1)} %convolution_convert_fusion) | data formatting | bytes 1048576 | tf_op jit(solution)/shard_map/reshape | solution.py:85
  3.3 6.3 %all-to-all-start = ((bf16[4,32,2,1024]{3,2,1,0:T(2,128)(2,1)}), bf16[4,32,2,1024]{3,2,1,0:T(2,128)(2,1)}, u32[]{:S(2)}, u32[]{:S(2)}) async-start(bf16[4,32,2,1024]{3,2,1,0:T(2,128)(2,1)} %reshape.152), calls=%async_computation | async-start | bytes 1048576 | tf_op jit(solution)/shard_map/all_to_all | solution.py:84
  9.6 0.0 copy-done.3
  9.6 0.0 copy-done.4
  9.6 0.2 convert_reduce_fusion
  9.8 0.1 broadcast_in_dim.3
  9.9 0.1 mul.105
  10.0 0.0 copy-done.2
  10.0 0.1 copy.42
  10.1 0.1 reshape.154
  10.2 0.2 convolution_convert_fusion.1
  10.4 24.2 %psum.7 = bf16[8,2,1024]{2,0,1:T(8,128)(2,1)S(1)} all-reduce(bf16[8,2,1024]{2,0,1:T(8,128)(2,1)S(1)} %bitcast.65), channel_id=1, replica_groups=mesh['chan'=8,'freq'=4] {'chan'}, use_global_device_ids=true, to_apply=%region_3.4 | all-reduce | flops 16384 | bytes 65536 | tf_op jit(solution)/shard_map/psum | solution.py:81
  34.6 13.8 %all_gather.3 = bf16[8,8,1024]{2,0,1:T(8,128)(2,1)S(1)} all-gather(bf16[8,2,1024]{2,0,1:T(8,128)(2,1)S(1)} %psum.7), channel_id=1, replica_groups=mesh['chan'=8,'freq'=4] {'freq'}, dimensions={1}, use_global_device_ids=true | all-gather | bytes 163840 | tf_op jit(solution)/shard_map/all_gather | solution.py:82
  48.4 0.0 copy-done.1
  48.4 0.5 multiply_reduce_fusion.1
  48.9 0.1 copy.71
  49.0 0.1 reshape.159
  49.3 0.0 all-to-all-done
  49.3 1.6 %copy.38 = bf16[1,32,4,2,1024]{4,3,2,1,0:T(2,128)(2,1)S(1)} copy(bf16[1,32,4,2,1024]{4,3,1,2,0:T(2,128)(2,1)} %bitcast.1) | data formatting | bytes 1048576 | tf_op jit(solution)/shard_map/all_to_all | solution.py:84
  50.8 1.0 %reshape.153 = bf16[32,8,1024]{2,1,0:T(8,128)(2,1)} reshape(bf16[1,32,4,2,1024]{4,3,2,1,0:T(2,128)(2,1)S(1)} %copy.38) | data formatting | bytes 1048576 | tf_op jit(solution)/shard_map/reshape | solution.py:87
  51.8 2.8 %multiply_reduce_fusion = (f32[32,1024]{1,0:T(8,128)S(1)}, f32[32,8,1024]{2,1,0:T(8,128)}) fusion(bf16[32,8,1024]{2,1,0:T(8,128)(2,1)} %reshape.153, bf16[1024,1024,1]{1,0,2:T(8,128)(2,1)S(1)} %copy-done.1), kind=kOutput, calls=%fused_computation.13 | convolution fusion | flops 537886720 | bytes 3801088 | tf_op jit(solution)/shard_map/cmw,wk->cmk/dot_general | solution.py:92
  54.7 0.1 reduce_sum.69
  54.8 0.2 reduce_sum.70
  55.0 1.6 %copy.70 = f32[32,8,4,2,128]{4,2,1,3,0:T(4,128)S(1)} copy(f32[32,8,4,2,128]{4,1,3,2,0:T(8,128)} %bitcast.59) | data formatting | bytes 2097152 | tf_op jit(solution)/shard_map/convert_element_type | solution.py:43
  56.6 0.4 reshape.158
  57.1 0.2 fusion.3
  57.2 0.0 copy-start.5
  57.3 0.1 slice_bitcast_fusion.1
  57.3 3.3 %add_reduce_fusion = (bf16[32,8,512]{2,1,0:T(8,128)(2,1)S(1)}, bf16[32,8,512]{2,1,0:T(8,128)(2,1)S(1)}) fusion(f32[8,8,512]{2,1,0:T(8,128)S(1)} %get-tuple-element.10, f32[32,8,512]{2,1,0:T(8,128)S(1)} %get-tuple-element.8, f32[8,8,512]{2,1,0:T(8,128)S(1)} %get-tuple-element.9, f32[32,8,512]{2,1,0:T(8,128)S(1)} %get-tuple-element.7), kind=kLoop, calls=%fused_computation.1 | loop fusion | flops 8126464 | bytes 1835008 | tf_op jit(solution)/shard_map/reduce_sum | solution.py:101
  60.6 0.0 copy-done.5
  60.6 0.4 convolution_convert_fusion.4
  61.1 0.8 copy.45
  61.9 1.0 %reshape.165 = bf16[4,2,16384]{2,1,0:T(2,128)(2,1)S(1)} reshape(bf16[512,8,32]{2,1,0:T(8,128)(2,1)S(1)} %bitcast.56) | data formatting | bytes 524288
  62.9 11.8 %all_to_all.35 = bf16[4,2,16384]{2,1,0:T(2,128)(2,1)S(1)} all-to-all(bf16[4,2,16384]{2,1,0:T(2,128)(2,1)S(1)} %reshape.165), channel_id=1, replica_groups=mesh['chan'=8,'freq'=4] {'freq'}, dimensions={0} | all-to-all | bytes 524288 | tf_op jit(solution)/shard_map/all_to_all | solution.py:108
  74.7 0.5 reshape.166
  75.2 0.6 copy.46
  75.8 0.3 fusion.1
  76.1 0.1 copy.50
  76.2 12.2 %all_to_all.36 = bf16[8,32,8,128]{3,2,1,0:T(8,128)(2,1)S(1)} all-to-all(bf16[8,32,8,128]{3,2,1,0:T(8,128)(2,1)S(1)} %bitcast.60), channel_id=1, replica_groups=mesh['chan'=8,'freq'=4] {'chan'}, dimensions={0} | all-to-all | bytes 1048576 | tf_op jit(solution)/shard_map/all_to_all | solution.py:116
  88.4 1.1 %bitcast_convert_fusion = f32[256,8,128]{2,1,0:T(8,128)} fusion(bf16[8,32,8,128]{3,2,1,0:T(8,128)(2,1)S(1)} %all_to_all.36), kind=kLoop, calls=%fused_computation.20 | loop fusion | flops 262144 | bytes 1572864 | tf_op jit(solution)/shard_map/convert_element_type | solution.py:117
  (8 shorter events, 0.1 us)
Async XLA Ops:
  0.0 1.1 %copy-start = (bf16[160,2048]{1,0:T(8,128)(2,1)S(1)}, bf16[160,2048]{1,0:T(8,128)(2,1)}, u32[]{:S(2)}) copy-start(bf16[160,2048]{1,0:T(8,128)(2,1)} %param.7) | copy-start | bytes 1966084
  0.0 48.4 %copy-start.1 = (bf16[1024,1024,1]{1,0,2:T(8,128)(2,1)S(1)}, bf16[1024,1024,1]{1,0,2:T(8,128)(2,1)}, u32[]{:S(2)}) copy-start(bf16[1024,1024,1]{1,0,2:T(8,128)(2,1)} %constant.56) | copy-start | bytes 6291460
  0.0 9.6 %copy-start.3 = (s32[4]{0:T(128)S(1)}, s32[4]{0:T(128)}, u32[]{:S(2)}) copy-start(s32[4]{0:T(128)} %param.10) | copy-start | bytes 52
  0.0 9.6 %copy-start.4 = (s32[128]{0:T(128)S(1)}, s32[128]{0:T(128)}, u32[]{:S(2)}) copy-start(s32[128]{0:T(128)} %param.9) | copy-start | bytes 1540
  1.1 8.9 %copy-start.2 = (s32[4,2]{0,1:T(2,128)S(1)}, s32[4,2]{0,1:T(2,128)}, u32[]{:S(2)}) copy-start(s32[4,2]{0,1:T(2,128)} %param.11) | copy-start | bytes 100
  3.3 45.9 %all-to-all-start = ((bf16[4,32,2,1024]{3,2,1,0:T(2,128)(2,1)}), bf16[4,32,2,1024]{3,2,1,0:T(2,128)(2,1)}, u32[]{:S(2)}, u32[]{:S(2)}) async-start(bf16[4,32,2,1024]{3,2,1,0:T(2,128)(2,1)} %reshape.152), calls=%async_computation | async-start | bytes 1048576 | tf_op jit(solution)/shard_map/all_to_all | solution.py:84
  57.2 3.4 %copy-start.5 = (bf16[1024,512,1]{1,0,2:T(8,128)(2,1)S(1)}, bf16[1024,512,1]{1,0,2:T(8,128)(2,1)}, u32[]{:S(2)}) copy-start(bf16[1024,512,1]{1,0,2:T(8,128)(2,1)} %constant.57) | copy-start | bytes 3145732

commit v2 on v1

--- a/solution.py
+++ b/solution.py
@@ -1,3 +1,4 @@
+import functools
 import math
 
 import jax
@@ -5,6 +6,8 @@
 import ml_dtypes
 import numpy as np
 from jax import lax
+from jax.experimental import pallas as pl
+from jax.experimental.pallas import tpu as pltpu
 from jax.sharding import PartitionSpec as P
 
 W = 1024
@@ -46,7 +49,7 @@
     return (values * factor).astype(jnp.bfloat16)
 
 
-def body(raw, good_list, dest, order, picks):
+def separate(raw, good_list, dest, order, picks):
     n_chan = lax.axis_size("chan")
     n_freq = lax.axis_size("freq")
     good_count = good_list.shape[0]
@@ -117,6 +120,319 @@
     return received.reshape(slot_count, sources, lags).astype(jnp.float32)
 
 
+MESH = pl.DeviceIdType.MESH
+CHUNKS = 2
+LANES = 128
+
+
+def column_order(bands):
+    return np.arange(W).reshape(bands, 2, W // bands // 2).transpose(1, 0, 2).reshape(W)
+
+
+def kernel(
+    n_chan,
+    n_freq,
+    order_ref,
+    picks_ref,
+    dest_ref,
+    good_ref,
+    raw_ref,
+    trans_hbm,
+    table_hbm,
+    out_ref,
+    trans_ref,
+    table_ref,
+    share_out,
+    share_in,
+    panel_out,
+    panel_in,
+    panel_raw,
+    spec_ref,
+    white_ref,
+    panel_ref,
+    cross_ref,
+    lag_out,
+    lag_in,
+    placed_ref,
+    local_sems,
+    share_send,
+    share_recv,
+    panel_send,
+    panel_recv,
+    gather_send,
+    gather_recv,
+    lag_send,
+    lag_recv,
+    place_send,
+    place_recv,
+):
+    f32, bf16 = jnp.float32, jnp.bfloat16
+    chan, freq = lax.axis_index("chan"), lax.axis_index("freq")
+    raw_rows = raw_ref.shape[0]
+    good_count = dest_ref.shape[1]
+    share = good_count // n_freq
+    capacity = 2 * good_count // n_chan
+    slot_count = n_chan * capacity
+    sub_count = raw_ref.shape[1] // W
+    total_sub = sub_count * n_freq
+    steps, per_step = picks_ref.shape
+    sources = steps * per_step
+    group = sources // CHUNKS
+    half = W // 2
+    lags = LAGS // n_freq
+
+    load_trans = pltpu.make_async_copy(trans_hbm, trans_ref, local_sems.at[0])
+    load_table = pltpu.make_async_copy(table_hbm, table_ref, local_sems.at[1])
+    load_trans.start()
+    load_table.start()
+
+    def chan_peer(d):
+        return lax.rem(chan + d, n_chan)
+
+    def freq_peer(d):
+        return lax.rem(freq + d, n_freq)
+
+    barrier = pltpu.get_barrier_semaphore()
+    for d in range(1, n_chan):
+        pl.semaphore_signal(barrier, inc=1, device_id={"chan": chan_peer(d)}, device_id_type=MESH)
+    for d in range(1, n_freq):
+        pl.semaphore_signal(barrier, inc=1, device_id={"freq": freq_peer(d)}, device_id_type=MESH)
+
+    good_col = jnp.transpose(
+        jnp.broadcast_to(good_ref[...].astype(f32), (good_count, good_count))
+    )[:, :1]
+    row_onehot = (
+        good_col == lax.broadcasted_iota(jnp.int32, (good_count, raw_rows), 1).astype(f32)
+    ).astype(bf16)
+    good = jnp.dot(row_onehot, raw_ref[...], preferred_element_type=f32).astype(bf16)
+    for f in range(n_freq):
+        share_out[f] = good[f * share : (f + 1) * share]
+    dest_row = jnp.broadcast_to(dest_ref[...].astype(f32), (good_count, good_count))
+    earlier = jnp.logical_and(
+        dest_row == jnp.transpose(dest_row),
+        lax.broadcasted_iota(jnp.int32, (good_count, good_count), 0)
+        < lax.broadcasted_iota(jnp.int32, (good_count, good_count), 1),
+    )
+    earlier_count = jnp.sum(jnp.where(earlier, 1.0, 0.0), axis=0, keepdims=True)
+    slot_index = dest_ref[...].astype(f32) * capacity + earlier_count
+
+    source_row = lax.broadcasted_iota(jnp.int32, (sources, good_count), 0)
+    source_slot = jnp.full((sources, good_count), -1, jnp.int32)
+    for t in range(steps):
+        for j in range(per_step):
+            pick = picks_ref[t, j]
+            slot = jnp.where(
+                lax.div(pick, capacity) == chan, order_ref[t] * capacity + lax.rem(pick, capacity), -1
+            )
+            source_slot = jnp.where(source_row == t * per_step + j, slot, source_slot)
+    source_onehot = (source_slot.astype(f32) == slot_index).astype(bf16)
+    chosen = jnp.dot(source_onehot, good, preferred_element_type=f32)
+    panel_out[...] = jnp.concatenate(
+        [chosen[:, m * W : (m + 1) * W] for m in range(sub_count)], axis=0
+    ).astype(bf16)
+
+    pl.semaphore_wait(barrier, n_chan + n_freq - 2)
+
+    pending = []
+
+    def send(src, dst, send_sem, recv_sem, peer):
+        copy = pltpu.make_async_remote_copy(
+            src_ref=src,
+            dst_ref=dst,
+            send_sem=send_sem,
+            recv_sem=recv_sem,
+            device_id=peer,
+            device_id_type=MESH,
+        )
+        copy.start()
+        pending.append(copy)
+        return copy
+
+    panel_copies = [
+        send(panel_out, panel_in.at[d - 1], panel_send.at[d - 1], panel_recv.at[d - 1],
+             {"chan": chan_peer(d)})
+        for d in range(1, n_chan)
+    ]
+    share_copies = [
+        send(share_out.at[freq_peer(d)], share_in.at[d - 1], share_send.at[d - 1],
+             share_recv.at[d - 1], {"freq": freq_peer(d)})
+        for d in range(1, n_freq)
+    ]
+    load_trans.wait()
+
+    def transform(rows, source):
+        stacked = jnp.concatenate([rows[:, m * W : (m + 1) * W] for m in range(sub_count)], axis=0)
+        spectra = jnp.dot(stacked, trans_ref[...], preferred_element_type=f32).astype(bf16)
+        for m in range(sub_count):
+            spec_ref[source * sub_count + m] = spectra[m * share : (m + 1) * share]
+
+    for copy in panel_copies:
+        copy.wait_recv()
+    total = panel_out[...].astype(f32)
+    for d in range(1, n_chan):
+        total = total + panel_in[d - 1].astype(f32)
+    panel_raw[freq] = total.astype(bf16)
+    gather_copies = [
+        send(panel_raw.at[freq], panel_raw.at[freq], gather_send.at[d - 1], gather_recv.at[d - 1],
+             {"freq": freq_peer(d)})
+        for d in range(1, n_freq)
+    ]
+    transform(share_out[freq], freq)
+    for d in range(1, n_freq):
+        share_copies[d - 1].wait_recv()
+        transform(share_in[d - 1], freq_peer(n_freq - d))
+    for copy in gather_copies:
+        copy.wait_recv()
+
+    def whiten_into(values, target):
+        re, im = values[..., :half], values[..., half:]
+        power = jnp.sum(re * re + im * im, axis=0, keepdims=True) * (1.0 / total_sub)
+        factor = 1.0 / jnp.sqrt(jnp.maximum(power, power_floor))
+        target[:, :, :half] = (re * factor).astype(bf16).astype(f32)
+        target[:, :, half:] = (im * factor).astype(bf16).astype(f32)
+
+    panel_spec = jnp.dot(
+        panel_raw[...].reshape(total_sub * sources, W), trans_ref[...], preferred_element_type=f32
+    ).astype(bf16).astype(f32)
+    whiten_into(panel_spec.reshape(total_sub, sources, W), panel_ref)
+    whiten_into(spec_ref[...].astype(f32), white_ref)
+    load_table.wait()
+
+    lag_copies = []
+    for h in range(CHUNKS):
+
+        def cross_bins(c, carry):
+            at_re = pl.ds(pl.multiple_of(c * LANES, LANES), LANES)
+            at_im = pl.ds(pl.multiple_of(half + c * LANES, LANES), LANES)
+            left_re, left_im = white_ref[:, :, at_re], white_ref[:, :, at_im]
+            for j in range(group):
+                source = h * group + j
+                right_re = panel_ref[:, source : source + 1, at_re]
+                right_im = panel_ref[:, source : source + 1, at_im]
+                real = jnp.sum(left_re * right_re + left_im * right_im, axis=0)
+                imag = jnp.sum(left_im * right_re - left_re * right_im, axis=0)
+                cross_ref[h, j * share : (j + 1) * share, at_re] = real.astype(bf16)
+                cross_ref[h, j * share : (j + 1) * share, at_im] = imag.astype(bf16)
+            return carry
+
+        lax.fori_loop(0, half // LANES, cross_bins, 0)
+        corr = jnp.dot(cross_ref[h], table_ref[...], preferred_element_type=f32).astype(bf16)
+        for f in range(n_freq):
+            lag_out[h, f] = corr[:, f * lags : (f + 1) * lags]
+        lag_copies.append([
+            send(lag_out.at[h, freq_peer(d)], lag_in.at[h, freq], lag_send.at[h, d - 1],
+                 lag_recv.at[h, d - 1], {"freq": freq_peer(d)})
+            for d in range(1, n_freq)
+        ])
+        lag_in[h, freq] = lag_out[h, freq]
+
+    slot_onehot = (
+        lax.broadcasted_iota(jnp.int32, (slot_count, good_count), 0).astype(f32) == slot_index
+    ).astype(bf16)
+    place_copies = []
+    own_copies = []
+    for h in range(CHUNKS):
+        for copy in lag_copies[h]:
+            copy.wait_recv()
+        corr = jnp.concatenate(
+            [
+                jnp.concatenate(
+                    [lag_in[h, f, j * share : (j + 1) * share] for f in range(n_freq)], axis=0
+                )
+                for j in range(group)
+            ],
+            axis=1,
+        )
+        placed = jnp.dot(slot_onehot, corr, preferred_element_type=f32).astype(bf16)
+        for b in range(n_chan):
+            placed_ref[h, b] = placed[b * capacity : (b + 1) * capacity]
+        at = pl.ds(h * group * lags, group * lags)
+        place_copies += [
+            send(placed_ref.at[h, chan_peer(d)], out_ref.at[chan, :, at], place_send.at[h, d - 1],
+                 place_recv.at[h, d - 1], {"chan": chan_peer(d)})
+            for d in range(1, n_chan)
+        ]
+        own = pltpu.make_async_copy(
+            placed_ref.at[h, chan], out_ref.at[chan, :, at], local_sems.at[2 + h]
+        )
+        own.start()
+        own_copies.append(own)
+    for copy in place_copies:
+        copy.wait_recv()
+    for own in own_copies:
+        own.wait()
+    for copy in pending:
+        copy.wait_send()
+
+
+def fused(raw, good_list, dest, order, picks):
+    n_chan = lax.axis_size("chan")
+    n_freq = lax.axis_size("freq")
+    good_count = good_list.shape[0]
+    share = good_count // n_freq
+    capacity = 2 * good_count // n_chan
+    sub_count = raw.shape[1] // W
+    total_sub = sub_count * n_freq
+    sources = picks.size
+    group = sources // CHUNKS
+    lags = LAGS // n_freq
+    columns = column_order(n_freq)
+    scale = 1.0 / math.sqrt(total_sub * (W // 2))
+    trans = jnp.asarray(transform_table(n_freq)[:, columns])
+    table = jnp.asarray(lag_rows(n_freq, scale)[columns])
+    bf16, f32 = jnp.bfloat16, jnp.float32
+    dma = pltpu.SemaphoreType.DMA
+    vmem = pl.BlockSpec(memory_space=pltpu.VMEM)
+    smem = pl.BlockSpec(memory_space=pltpu.SMEM)
+    hbm = pl.BlockSpec(memory_space=pl.ANY)
+    received = pl.pallas_call(
+        functools.partial(kernel, n_chan, n_freq),
+        out_shape=jax.ShapeDtypeStruct((n_chan, capacity, sources * lags), bf16),
+        in_specs=[smem, smem, vmem, vmem, vmem, hbm, hbm],
+        out_specs=hbm,
+        scratch_shapes=[
+            pltpu.VMEM((W, W), bf16),
+            pltpu.VMEM((W, LAGS), bf16),
+            pltpu.VMEM((n_freq, share, sub_count * W), bf16),
+            pltpu.VMEM((n_freq - 1, share, sub_count * W), bf16),
+            pltpu.VMEM((sub_count * sources, W), bf16),
+            pltpu.VMEM((n_chan - 1, sub_count * sources, W), bf16),
+            pltpu.VMEM((n_freq, sub_count * sources, W), bf16),
+            pltpu.VMEM((total_sub, share, W), bf16),
+            pltpu.VMEM((total_sub, share, W), f32),
+            pltpu.VMEM((total_sub, sources, W), f32),
+            pltpu.VMEM((CHUNKS, group * share, W), bf16),
+            pltpu.VMEM((CHUNKS, n_freq, group * share, lags), bf16),
+            pltpu.VMEM((CHUNKS, n_freq, group * share, lags), bf16),
+            pltpu.VMEM((CHUNKS, n_chan, capacity, group * lags), bf16),
+            dma((2 + CHUNKS,)),
+            dma((n_freq - 1,)),
+            dma((n_freq - 1,)),
+            dma((n_chan - 1,)),
+            dma((n_chan - 1,)),
+            dma((n_freq - 1,)),
+            dma((n_freq - 1,)),
+            dma((CHUNKS, n_freq - 1)),
+            dma((CHUNKS, n_freq - 1)),
+            dma((CHUNKS, n_chan - 1)),
+            dma((CHUNKS, n_chan - 1)),
+        ],
+        compiler_params=pltpu.CompilerParams(
+            collective_id=0, has_side_effects=True, vmem_limit_bytes=40 * 1024 * 1024
+        ),
+    )(order, picks, dest.reshape(1, good_count), good_list.reshape(1, good_count), raw, trans, table)
+    return received.reshape(n_chan * capacity, sources, lags).astype(f32)
+
+
+def body(raw, good_list, dest, order, picks):
+    n_chan = lax.axis_size("chan")
+    n_freq = lax.axis_size("freq")
+    capacity = 2 * good_list.shape[0] // n_chan
+    if capacity % 16 == 0 and n_chan <= 16 and good_list.shape[0] == LANES:
+        return fused(raw, good_list, dest, order, picks)
+    return separate(raw, good_list, dest, order, picks)
+
+
 def solution(mesh):
     placed = (P("chan", "freq"), P("chan"), P("chan"), P(), P())
     return jax.shard_map(

time: 89.9 us -> 42.3 us (0.47)
  blocking collectives: 62 us -> 0 us
  Pallas kernels: 0 us -> 34.3 us
  starting transfers between devices: 6.32 us -> 0 us
  matrix products: 5.27 us -> 0 us
  other arithmetic: 4.92 us -> 0 us
  local copies, waits for them, and re-layouts: 10.7 us -> 7.72 us
    pallas_call x0 -> x1, Pallas kernels: none -> 34.3 us  [fused(): pl.pallas_call(functools.partial(kernel, n_chan, n_freq), out_shape=jax.S...]
    psum x1 -> x0, blocking collectives: 24.2 us -> none  [body(): panel_raw = lax.psum(panel_raw, 'chan')]
    all_to_all x2 -> x0, blocking collectives: 24 us -> none  [the longest x1 12.2 us: body(): lax.all_to_all(placed, 'chan', split_axis=0, concat_axis=0, tiled=True)]
    all_gather x1 -> x0, blocking collectives: 13.8 us -> none  [body(): lax.all_gather(panel_raw.reshape(sources, sub_count, W), 'freq', axis=1,...]
    all_to_all x1 -> x0, starting transfers between devices: 6.32 us -> none  [body(): lax.all_to_all(good.reshape(n_freq, share, sub_count, W), 'freq', split_a...]
    dot_general x6 -> x0, matrix products: 5.27 us -> none  [the longest x2 3.32 us: white(): jnp.einsum('cmw,wk->cmk', values, trans, preferred_element_type=jnp.float32)]
    unnamed x16 -> x14, local copies, waits for them, and re-layouts: 2.77 us -> 7.72 us
    reduce_sum x4 -> x0, other arithmetic: 3.61 us -> none  [the longest x1 3.26 us: body(): real_part = jnp.sum(left_re * right_re + left_im * right_im, axis=2)]
  transfers between devices with their start and end apart: 1 -> 0, of which waited for: 0 -> 0; matrix products, arithmetic and copies ran while one was open for 2% -> 0% of each run, Pallas kernels for 0% -> 0%
where the time goes in v2:
time: 42.3 us; the launch traced here: 42 us
  Pallas kernels  34.3 us (81%)
  local copies, waits for them, and re-layouts  7.72 us (18%)
    pallas_call x1, Pallas kernels, fused(): pl.pallas_call(functools.partial(kernel, n_chan, n_freq), out_shape=jax.S...  34.3 us
    unnamed x14, local copies, waits for them, and re-layouts  7.72 us

profile of v2, /device:TPU:0, one launch (start us, length us, event | category | flops | bytes accessed | tf_op | source)
XLA Modules:
  0.0 42.0 jit_solution(11285552941427812391)
XLA Ops:
  0.0 0.8 %copy.8.picks_ref = s32[4,2]{1,0:T(4,128)S(1)} copy(s32[4,2]{0,1:T(2,128)} %param.11) | data formatting | bytes 64 | tf_op args[4]
  0.8 0.0 copy-start
  0.8 1.6 %copy-done = bf16[1024,1024]{1,0:T(8,128)(2,1)S(1)} copy-done((bf16[1024,1024]{1,0:T(8,128)(2,1)S(1)}, bf16[1024,1024]{1,0:T(8,128)(2,1)}, u32[]{:S(2)}) %copy-start) | copy-done | bytes 2097176
  2.4 0.0 copy-start.1
  2.4 1.2 %copy-done.1 = bf16[1024,512]{1,0:T(8,128)(2,1)S(1)} copy-done((bf16[1024,512]{1,0:T(8,128)(2,1)S(1)}, bf16[1024,512]{1,0:T(8,128)(2,1)}, u32[]{:S(2)}) %copy-start.1) | copy-done | bytes 1048600
  3.6 0.0 copy-start.2
  3.6 1.1 %copy-done.2 = bf16[160,2048]{1,0:T(8,128)(2,1)S(1)} copy-done((bf16[160,2048]{1,0:T(8,128)(2,1)S(1)}, bf16[160,2048]{1,0:T(8,128)(2,1)}, u32[]{:S(2)}) %copy-start.2) | copy-done | bytes 655384
  4.7 0.0 copy-start.3
  4.7 0.7 %copy-done.3 = s32[4]{0:T(128)S(1)} copy-done((s32[4]{0:T(128)S(1)}, s32[4]{0:T(128)}, u32[]{:S(2)}) %copy-start.3) | copy-done | bytes 40
  5.3 0.0 copy-start.4
  5.3 0.7 %copy-done.4 = s32[128]{0:T(128)S(1)} copy-done((s32[128]{0:T(128)S(1)}, s32[128]{0:T(128)}, u32[]{:S(2)}) %copy-start.4) | copy-done | bytes 536
  6.0 0.0 copy-start.5
  6.0 0.7 %copy-done.5 = s32[128]{0:T(128)S(1)} copy-done((s32[128]{0:T(128)S(1)}, s32[128]{0:T(128)}, u32[]{:S(2)}) %copy-start.5) | copy-done | bytes 536
  6.6 34.3 %shard_map.73 = bf16[8,32,1024]{2,1,0:T(8,128)(2,1)S(1)} custom-call(s32[4]{0:T(128)S(1)} %copy-done.3, s32[4,2]{1,0:T(4,128)S(1)} %copy.8.picks_ref, s32[1,128]{1,0:T(1,128)S(1)} %bitcast.7, s32[1,128]{1,0:T(1,128)S(1)} %bitcast.8, bf16[160,2048]{1,0:T(8,128)(2,1)S(1)} %copy-done.2, bf16[1024,1024]{1,0:T(8,128)(2,1)S(1)} %copy-done, ...), custom_call_target="tpu_custom_call" | custom-call | tf_op jit(solution)/shard_map/pallas_call | solution.py:388
  40.9 1.1 %copy.9 = f32[32,8,8,128]{3,2,1,0:T(8,128)} copy(bf16[32,8,8,128]{3,1,2,0:T(8,128)(2,1)S(1)} %bitcast.6) | data formatting | bytes 1572864
Async XLA Ops:
  0.8 1.6 %copy-start = (bf16[1024,1024]{1,0:T(8,128)(2,1)S(1)}, bf16[1024,1024]{1,0:T(8,128)(2,1)}, u32[]{:S(2)}) copy-start(bf16[1024,1024]{1,0:T(8,128)(2,1)} %constant.4.clone.trans_hbm) | copy-start | bytes 6291460
  2.4 1.2 %copy-start.1 = (bf16[1024,512]{1,0:T(8,128)(2,1)S(1)}, bf16[1024,512]{1,0:T(8,128)(2,1)}, u32[]{:S(2)}) copy-start(bf16[1024,512]{1,0:T(8,128)(2,1)} %constant.5.clone.table_hbm) | copy-start | bytes 3145732
  3.6 1.1 %copy-start.2 = (bf16[160,2048]{1,0:T(8,128)(2,1)S(1)}, bf16[160,2048]{1,0:T(8,128)(2,1)}, u32[]{:S(2)}) copy-start(bf16[160,2048]{1,0:T(8,128)(2,1)} %raw_ref.1) | copy-start | bytes 1966084
  4.7 0.7 %copy-start.3 = (s32[4]{0:T(128)S(1)}, s32[4]{0:T(128)}, u32[]{:S(2)}) copy-start(s32[4]{0:T(128)} %order_ref.1) | copy-start | bytes 52
  5.3 0.7 %copy-start.4 = (s32[128]{0:T(128)S(1)}, s32[128]{0:T(128)}, u32[]{:S(2)}) copy-start(s32[128]{0:T(128)} %param.9) | copy-start | bytes 1540
  6.0 0.7 %copy-start.5 = (s32[128]{0:T(128)S(1)}, s32[128]{0:T(128)}, u32[]{:S(2)}) copy-start(s32[128]{0:T(128)} %param.8) | copy-start | bytes 1540

commit v3 on v2

--- a/solution.py
+++ b/solution.py
@@ -132,14 +132,19 @@
 def kernel(
     n_chan,
     n_freq,
+    order_hbm,
+    picks_hbm,
+    dest_hbm,
+    good_hbm,
+    raw_hbm,
+    trans_hbm,
+    table_hbm,
+    out_ref,
     order_ref,
     picks_ref,
     dest_ref,
     good_ref,
     raw_ref,
-    trans_hbm,
-    table_hbm,
-    out_ref,
     trans_ref,
     table_ref,
     share_out,
@@ -175,12 +180,24 @@
     slot_count = n_chan * capacity
     sub_count = raw_ref.shape[1] // W
     total_sub = sub_count * n_freq
-    steps, per_step = picks_ref.shape
+    per_step, steps = picks_ref.shape
     sources = steps * per_step
     group = sources // CHUNKS
     half = W // 2
     lags = LAGS // n_freq
 
+    loads = [
+        pltpu.make_async_copy(source, target, local_sems.at[2 + CHUNKS + i])
+        for i, (source, target) in enumerate((
+            (raw_hbm, raw_ref),
+            (good_hbm, good_ref),
+            (dest_hbm, dest_ref),
+            (order_hbm, order_ref),
+            (picks_hbm, picks_ref),
+        ))
+    ]
+    for load in loads:
+        load.start()
     load_trans = pltpu.make_async_copy(trans_hbm, trans_ref, local_sems.at[0])
     load_table = pltpu.make_async_copy(table_hbm, table_ref, local_sems.at[1])
     load_trans.start()
@@ -197,6 +214,9 @@
         pl.semaphore_signal(barrier, inc=1, device_id={"chan": chan_peer(d)}, device_id_type=MESH)
     for d in range(1, n_freq):
         pl.semaphore_signal(barrier, inc=1, device_id={"freq": freq_peer(d)}, device_id_type=MESH)
+
+    for load in loads:
+        load.wait()
 
     good_col = jnp.transpose(
         jnp.broadcast_to(good_ref[...].astype(f32), (good_count, good_count))
@@ -220,7 +240,7 @@
     source_slot = jnp.full((sources, good_count), -1, jnp.int32)
     for t in range(steps):
         for j in range(per_step):
-            pick = picks_ref[t, j]
+            pick = picks_ref[j, t]
             slot = jnp.where(
                 lax.div(pick, capacity) == chan, order_ref[t] * capacity + lax.rem(pick, capacity), -1
             )
@@ -382,15 +402,18 @@
     table = jnp.asarray(lag_rows(n_freq, scale)[columns])
     bf16, f32 = jnp.bfloat16, jnp.float32
     dma = pltpu.SemaphoreType.DMA
-    vmem = pl.BlockSpec(memory_space=pltpu.VMEM)
-    smem = pl.BlockSpec(memory_space=pltpu.SMEM)
-    hbm = pl.BlockSpec(memory_space=pl.ANY)
+    hbm = pl.BlockSpec(memory_space=pltpu.HBM)
     received = pl.pallas_call(
         functools.partial(kernel, n_chan, n_freq),
         out_shape=jax.ShapeDtypeStruct((n_chan, capacity, sources * lags), bf16),
-        in_specs=[smem, smem, vmem, vmem, vmem, hbm, hbm],
-        out_specs=hbm,
+        in_specs=[hbm] * 7,
+        out_specs=pl.BlockSpec(memory_space=pl.ANY),
         scratch_shapes=[
+            pltpu.SMEM(order.shape, jnp.int32),
+            pltpu.SMEM(picks.shape[::-1], jnp.int32),
+            pltpu.VMEM((1, good_count), jnp.int32),
+            pltpu.VMEM((1, good_count), jnp.int32),
+            pltpu.VMEM(raw.shape, bf16),
             pltpu.VMEM((W, W), bf16),
             pltpu.VMEM((W, LAGS), bf16),
             pltpu.VMEM((n_freq, share, sub_count * W), bf16),
@@ -405,7 +428,7 @@
             pltpu.VMEM((CHUNKS, n_freq, group * share, lags), bf16),
             pltpu.VMEM((CHUNKS, n_freq, group * share, lags), bf16),
             pltpu.VMEM((CHUNKS, n_chan, capacity, group * lags), bf16),
-            dma((2 + CHUNKS,)),
+            dma((7 + CHUNKS,)),
             dma((n_freq - 1,)),
             dma((n_freq - 1,)),
             dma((n_chan - 1,)),
@@ -418,9 +441,9 @@
             dma((CHUNKS, n_chan - 1)),
         ],
         compiler_params=pltpu.CompilerParams(
-            collective_id=0, has_side_effects=True, vmem_limit_bytes=40 * 1024 * 1024
+            collective_id=0, has_side_effects=True, vmem_limit_bytes=63 * 1024 * 1024
         ),
-    )(order, picks, dest.reshape(1, good_count), good_list.reshape(1, good_count), raw, trans, table)
+    )(order, picks.T, dest.reshape(1, good_count), good_list.reshape(1, good_count), raw, trans, table)
     return received.reshape(n_chan * capacity, sources, lags).astype(f32)
 
 

time: 42.3 us -> 35.9 us (0.85)
  local copies, waits for them, and re-layouts: 7.72 us -> 2.13 us
  Pallas kernels: 34.3 us -> 33.6 us
    unnamed x14 -> x1, local copies, waits for them, and re-layouts: 7.72 us -> 2.13 us
    pallas_call x1, Pallas kernels: 34.3 us -> 33.6 us  [fused(): pl.pallas_call(functools.partial(kernel, n_chan, n_freq), out_shape=jax.S...]
where the time goes in v3:
time: 35.9 us; the launch traced here: 35.7 us
  Pallas kernels  33.6 us (94%)
  local copies, waits for them, and re-layouts  2.13 us (6%)
    pallas_call x1, Pallas kernels, fused(): pl.pallas_call(functools.partial(kernel, n_chan, n_freq), out_shape=jax.S...  33.6 us
    unnamed x1, local copies, waits for them, and re-layouts  2.13 us

profile of v3, /device:TPU:0, one launch (start us, length us, event | category | flops | bytes accessed | tf_op | source)
XLA Modules:
  0.0 35.7 jit_solution(7992661065044593072)
XLA Ops:
  0.0 33.6 %shard_map.73 = bf16[8,32,1024]{2,1,0:T(8,128)(2,1)} custom-call(s32[4]{0:T(128)} %order_hbm.1, s32[2,4]{1,0:T(2,128)} %bitcast.8, s32[1,128]{1,0:T(1,128)} %bitcast.9, s32[1,128]{1,0:T(1,128)} %bitcast.10, bf16[160,2048]{1,0:T(8,128)(2,1)} %raw_hbm.1, bf16[1024,1024]{1,0:T(8,128)(2,1)} %constant.4.clone.trans_hbm, bf16[1024,512]{1,0:T(8,128)(2,1)} %constant.5.clone.table_hbm), custom_call_target="tpu_custom_call" | custom-call | tf_op jit(solution)/shard_map/pallas_call | solution.py:406
  33.6 2.1 %copy.8 = f32[32,8,8,128]{3,2,1,0:T(8,128)} copy(bf16[32,8,8,128]{3,1,2,0:T(8,128)(2,1)} %bitcast.7) | data formatting | bytes 1572864

commit v4 on v3

--- a/solution.py
+++ b/solution.py
@@ -122,6 +122,7 @@
 
 MESH = pl.DeviceIdType.MESH
 CHUNKS = 2
+PORTIONS = 1
 LANES = 128
 
 
@@ -152,7 +153,6 @@
     panel_out,
     panel_in,
     panel_raw,
-    spec_ref,
     white_ref,
     panel_ref,
     cross_ref,
@@ -176,6 +176,7 @@
     raw_rows = raw_ref.shape[0]
     good_count = dest_ref.shape[1]
     share = good_count // n_freq
+    portion = share // PORTIONS
     capacity = 2 * good_count // n_chan
     slot_count = n_chan * capacity
     sub_count = raw_ref.shape[1] // W
@@ -225,8 +226,10 @@
         good_col == lax.broadcasted_iota(jnp.int32, (good_count, raw_rows), 1).astype(f32)
     ).astype(bf16)
     good = jnp.dot(row_onehot, raw_ref[...], preferred_element_type=f32).astype(bf16)
-    for f in range(n_freq):
-        share_out[f] = good[f * share : (f + 1) * share]
+    for g in range(PORTIONS):
+        for f in range(n_freq):
+            first = f * share + g * portion
+            share_out[g, f] = good[first : first + portion]
     dest_row = jnp.broadcast_to(dest_ref[...].astype(f32), (good_count, good_count))
     earlier = jnp.logical_and(
         dest_row == jnp.transpose(dest_row),
@@ -273,19 +276,16 @@
              {"chan": chan_peer(d)})
         for d in range(1, n_chan)
     ]
-    share_copies = [
-        send(share_out.at[freq_peer(d)], share_in.at[d - 1], share_send.at[d - 1],
-             share_recv.at[d - 1], {"freq": freq_peer(d)})
-        for d in range(1, n_freq)
-    ]
-    load_trans.wait()
-
-    def transform(rows, source):
-        stacked = jnp.concatenate([rows[:, m * W : (m + 1) * W] for m in range(sub_count)], axis=0)
-        spectra = jnp.dot(stacked, trans_ref[...], preferred_element_type=f32).astype(bf16)
-        for m in range(sub_count):
-            spec_ref[source * sub_count + m] = spectra[m * share : (m + 1) * share]
-
+    def send_shares(g):
+        return [
+            send(share_out.at[g, freq_peer(d)], share_in.at[g, freq], share_send.at[g, d - 1],
+                 share_recv.at[g, d - 1], {"freq": freq_peer(d)})
+            for d in range(1, n_freq)
+        ]
+
+    share_copies = [send_shares(g) for g in range(PORTIONS)]
+    for g in range(PORTIONS):
+        share_in[g, freq] = share_out[g, freq]
     for copy in panel_copies:
         copy.wait_recv()
     total = panel_out[...].astype(f32)
@@ -297,12 +297,7 @@
              {"freq": freq_peer(d)})
         for d in range(1, n_freq)
     ]
-    transform(share_out[freq], freq)
-    for d in range(1, n_freq):
-        share_copies[d - 1].wait_recv()
-        transform(share_in[d - 1], freq_peer(n_freq - d))
-    for copy in gather_copies:
-        copy.wait_recv()
+    load_trans.wait()
 
     def whiten_into(values, target):
         re, im = values[..., :half], values[..., half:]
@@ -311,40 +306,63 @@
         target[:, :, :half] = (re * factor).astype(bf16).astype(f32)
         target[:, :, half:] = (im * factor).astype(bf16).astype(f32)
 
+    def transform(g):
+        for copy in share_copies[g]:
+            copy.wait_recv()
+        stacked = jnp.concatenate(
+            [
+                share_in[g, f, :, m * W : (m + 1) * W]
+                for f in range(n_freq)
+                for m in range(sub_count)
+            ],
+            axis=0,
+        )
+        spectra = jnp.dot(stacked, trans_ref[...], preferred_element_type=f32).astype(bf16)
+        whiten_into(spectra.astype(f32).reshape(total_sub, portion, W), white_ref.at[g])
+
+    lag_copies = []
+
+    def lag_part(g, first, count):
+        def cross_bins(c, carry):
+            at_re = pl.ds(pl.multiple_of(c * LANES, LANES), LANES)
+            at_im = pl.ds(pl.multiple_of(half + c * LANES, LANES), LANES)
+            left_re, left_im = white_ref[g, :, :, at_re], white_ref[g, :, :, at_im]
+            for j in range(first, first + count):
+                right_re = panel_ref[:, j : j + 1, at_re]
+                right_im = panel_ref[:, j : j + 1, at_im]
+                real = jnp.sum(left_re * right_re + left_im * right_im, axis=0)
+                imag = jnp.sum(left_im * right_re - left_re * right_im, axis=0)
+                cross_ref[g, j * portion : (j + 1) * portion, at_re] = real.astype(bf16)
+                cross_ref[g, j * portion : (j + 1) * portion, at_im] = imag.astype(bf16)
+            return carry
+
+        lax.fori_loop(0, half // LANES, cross_bins, 0)
+        rows = slice(first * portion, (first + count) * portion)
+        at = pl.ds(first * portion, count * portion)
+        part = len(lag_copies)
+        corr = jnp.dot(cross_ref[g, rows], table_ref[...], preferred_element_type=f32).astype(bf16)
+        for f in range(n_freq):
+            lag_out[g, f, rows] = corr[:, f * lags : (f + 1) * lags]
+        lag_copies.append([
+            send(lag_out.at[g, freq_peer(d), at], lag_in.at[g, freq, at], lag_send.at[part, d - 1],
+                 lag_recv.at[part, d - 1], {"freq": freq_peer(d)})
+            for d in range(1, n_freq)
+        ])
+        lag_in[g, freq, rows] = lag_out[g, freq, rows]
+
+    transform(0)
+    for copy in gather_copies:
+        copy.wait_recv()
     panel_spec = jnp.dot(
         panel_raw[...].reshape(total_sub * sources, W), trans_ref[...], preferred_element_type=f32
     ).astype(bf16).astype(f32)
     whiten_into(panel_spec.reshape(total_sub, sources, W), panel_ref)
-    whiten_into(spec_ref[...].astype(f32), white_ref)
     load_table.wait()
-
-    lag_copies = []
+    for g in range(PORTIONS - 1):
+        lag_part(g, 0, sources)
+        transform(g + 1)
     for h in range(CHUNKS):
-
-        def cross_bins(c, carry):
-            at_re = pl.ds(pl.multiple_of(c * LANES, LANES), LANES)
-            at_im = pl.ds(pl.multiple_of(half + c * LANES, LANES), LANES)
-            left_re, left_im = white_ref[:, :, at_re], white_ref[:, :, at_im]
-            for j in range(group):
-                source = h * group + j
-                right_re = panel_ref[:, source : source + 1, at_re]
-                right_im = panel_ref[:, source : source + 1, at_im]
-                real = jnp.sum(left_re * right_re + left_im * right_im, axis=0)
-                imag = jnp.sum(left_im * right_re - left_re * right_im, axis=0)
-                cross_ref[h, j * share : (j + 1) * share, at_re] = real.astype(bf16)
-                cross_ref[h, j * share : (j + 1) * share, at_im] = imag.astype(bf16)
-            return carry
-
-        lax.fori_loop(0, half // LANES, cross_bins, 0)
-        corr = jnp.dot(cross_ref[h], table_ref[...], preferred_element_type=f32).astype(bf16)
-        for f in range(n_freq):
-            lag_out[h, f] = corr[:, f * lags : (f + 1) * lags]
-        lag_copies.append([
-            send(lag_out.at[h, freq_peer(d)], lag_in.at[h, freq], lag_send.at[h, d - 1],
-                 lag_recv.at[h, d - 1], {"freq": freq_peer(d)})
-            for d in range(1, n_freq)
-        ])
-        lag_in[h, freq] = lag_out[h, freq]
+        lag_part(PORTIONS - 1, h * group, group)
 
     slot_onehot = (
         lax.broadcasted_iota(jnp.int32, (slot_count, good_count), 0).astype(f32) == slot_index
@@ -352,14 +370,20 @@
     place_copies = []
     own_copies = []
     for h in range(CHUNKS):
-        for copy in lag_copies[h]:
-            copy.wait_recv()
+        for part in range(PORTIONS - 1 + h if h else 0, PORTIONS + h):
+            for copy in lag_copies[part]:
+                copy.wait_recv()
         corr = jnp.concatenate(
             [
                 jnp.concatenate(
-                    [lag_in[h, f, j * share : (j + 1) * share] for f in range(n_freq)], axis=0
+                    [
+                        lag_in[g, f, j * portion : (j + 1) * portion]
+                        for f in range(n_freq)
+                        for g in range(PORTIONS)
+                    ],
+                    axis=0,
                 )
-                for j in range(group)
+                for j in range(h * group, (h + 1) * group)
             ],
             axis=1,
         )
@@ -395,6 +419,7 @@
     total_sub = sub_count * n_freq
     sources = picks.size
     group = sources // CHUNKS
+    portion = share // PORTIONS
     lags = LAGS // n_freq
     columns = column_order(n_freq)
     scale = 1.0 / math.sqrt(total_sub * (W // 2))
@@ -416,27 +441,26 @@
             pltpu.VMEM(raw.shape, bf16),
             pltpu.VMEM((W, W), bf16),
             pltpu.VMEM((W, LAGS), bf16),
-            pltpu.VMEM((n_freq, share, sub_count * W), bf16),
-            pltpu.VMEM((n_freq - 1, share, sub_count * W), bf16),
+            pltpu.VMEM((PORTIONS, n_freq, portion, sub_count * W), bf16),
+            pltpu.VMEM((PORTIONS, n_freq, portion, sub_count * W), bf16),
             pltpu.VMEM((sub_count * sources, W), bf16),
             pltpu.VMEM((n_chan - 1, sub_count * sources, W), bf16),
             pltpu.VMEM((n_freq, sub_count * sources, W), bf16),
-            pltpu.VMEM((total_sub, share, W), bf16),
-            pltpu.VMEM((total_sub, share, W), f32),
+            pltpu.VMEM((PORTIONS, total_sub, portion, W), f32),
             pltpu.VMEM((total_sub, sources, W), f32),
-            pltpu.VMEM((CHUNKS, group * share, W), bf16),
-            pltpu.VMEM((CHUNKS, n_freq, group * share, lags), bf16),
-            pltpu.VMEM((CHUNKS, n_freq, group * share, lags), bf16),
+            pltpu.VMEM((PORTIONS, sources * portion, W), bf16),
+            pltpu.VMEM((PORTIONS, n_freq, sources * portion, lags), bf16),
+            pltpu.VMEM((PORTIONS, n_freq, sources * portion, lags), bf16),
             pltpu.VMEM((CHUNKS, n_chan, capacity, group * lags), bf16),
             dma((7 + CHUNKS,)),
-            dma((n_freq - 1,)),
-            dma((n_freq - 1,)),
+            dma((PORTIONS, n_freq - 1)),
+            dma((PORTIONS, n_freq - 1)),
             dma((n_chan - 1,)),
             dma((n_chan - 1,)),
             dma((n_freq - 1,)),
             dma((n_freq - 1,)),
-            dma((CHUNKS, n_freq - 1)),
-            dma((CHUNKS, n_freq - 1)),
+            dma((PORTIONS - 1 + CHUNKS, n_freq - 1)),
+            dma((PORTIONS - 1 + CHUNKS, n_freq - 1)),
             dma((CHUNKS, n_chan - 1)),
             dma((CHUNKS, n_chan - 1)),
         ],

time: 35.9 us -> 35.6 us (level)
  no operation moved by 1% of the time
where the time goes in v4:
time: 35.6 us; the launch traced here: 35.4 us
  Pallas kernels  33.3 us (94%)
  local copies, waits for them, and re-layouts  2.13 us (6%)
    pallas_call x1, Pallas kernels, fused(): pl.pallas_call(functools.partial(kernel, n_chan, n_freq), out_shape=jax.S...  33.3 us
    unnamed x1, local copies, waits for them, and re-layouts  2.13 us

profile of v4, /device:TPU:0, one launch (start us, length us, event | category | flops | bytes accessed | tf_op | source)
XLA Modules:
  0.0 35.4 jit_solution(11421588609504164386)
XLA Ops:
  0.0 33.3 %shard_map.73 = bf16[8,32,1024]{2,1,0:T(8,128)(2,1)} custom-call(s32[4]{0:T(128)} %order_hbm.1, s32[2,4]{1,0:T(2,128)} %bitcast.8, s32[1,128]{1,0:T(1,128)} %bitcast.9, s32[1,128]{1,0:T(1,128)} %bitcast.10, bf16[160,2048]{1,0:T(8,128)(2,1)} %raw_hbm.1, bf16[1024,1024]{1,0:T(8,128)(2,1)} %constant.4.clone.trans_hbm, bf16[1024,512]{1,0:T(8,128)(2,1)} %constant.5.clone.table_hbm), custom_call_target="tpu_custom_call" | custom-call | tf_op jit(solution)/shard_map/pallas_call | solution.py:431
  33.3 2.1 %copy.8 = f32[32,8,8,128]{3,2,1,0:T(8,128)} copy(bf16[32,8,8,128]{3,1,2,0:T(8,128)(2,1)} %bitcast.7) | data formatting | bytes 1572864
